TPU v7x, 32 devices: a whole 2x2x4 slice. The times are simulated.
32 devices in a mesh: seq: 4 (over x, core), head: 4 (over z), batch: 2 (over y).
Axes of the slice: x: 2, y: 2, z: 4, core: 2. Of those that a mesh axis runs over, the one named last changes fastest.
Arguments:
- hyena_inputs: bfloat16 [4096, 3, 8192], P(('batch', 'seq'), None, 'head'), parts along dimension 0, may hold values from -6 to 6
- short_filter: float32 [3, 3, 8192], P(None, None, 'head'), may hold values from -3.5 to 3.5
- medium_filter: float32 [128, 8192], P(None, 'head'), may hold values from -0.5 to 0.5
- q_proj: bfloat16 [4096, 8192], P(('batch', 'seq'), 'head'), parts along dimension 0, may hold values from -8 to 8
- k_proj: bfloat16 [4096, 8192], P(('batch', 'seq'), 'head'), parts along dimension 0, may hold values from -8 to 8
- out_weight: bfloat16 [8192, 8192], P('head'), may hold values from -0.25 to 0.25
Outputs:
- hyena_out: bfloat16 [4096, 8192], P(('batch', 'seq'), 'head'), parts along dimension 0
- mixed: bfloat16 [4096, 8192], P(('batch', 'seq'), 'head'), parts along dimension 0
There are 2 independent parts, one for each index of `batch`. A program takes and returns all parts, laid end to end along the dimension named above; an argument that names none is the same for every part. Nothing has to cross between parts.
All inputs are finite; a program needn't handle non-finite values.
Results may differ from a plain program's by a relative error of at most 0.011.
Values may be sent and summed in bfloat16 or wider, within the bound.
A program may use at most 192 MiB of HBM per device.

v0:
```python
import math
import jax
import jax.numpy as jnp
from jax import lax
from jax.sharding import PartitionSpec as P

HEAD_SIZE = 128


def passed_along(x, axis, by):
    length = lax.axis_size(axis)
    pairs = [(i, i + by) for i in range(length) if 0 <= i + by < length]
    return lax.ppermute(x, axis, pairs)


def causal_depthwise(extended, taps, out_rows):
    tap_count = taps.shape[0]
    window = extended[extended.shape[0] - out_rows - tap_count + 1 :]
    kernel = taps[::-1][:, None, :]
    result = lax.conv_general_dilated(
        window[None],
        kernel,
        (1,),
        "VALID",
        feature_group_count=extended.shape[1],
        dimension_numbers=("NWC", "WIO", "NWC"),
        precision=lax.Precision.HIGHEST,
    )
    return result[0]


def per_device(hyena_inputs, short_filter, medium_filter, q_proj, k_proj, out_weight):
    tok_rows = hyena_inputs.shape[0]
    chan_width = hyena_inputs.shape[2]
    short_taps = short_filter.shape[1]
    med_taps = medium_filter.shape[0]
    short_table = jnp.transpose(short_filter, (1, 0, 2)).reshape(short_taps, 3 * chan_width)
    input_margin = passed_along(hyena_inputs[tok_rows - (short_taps - 1) :], "seq", 1)
    joined = (
        jnp.concatenate([input_margin, hyena_inputs], 0)
        .astype(jnp.float32)
        .reshape(-1, 3 * chan_width)
    )
    filtered = causal_depthwise(joined, short_table, tok_rows).reshape(tok_rows, 3, chan_width)
    product = (filtered[:, 1] * filtered[:, 2]).astype(jnp.bfloat16)
    product_margin = passed_along(product[tok_rows - (med_taps - 1) :], "seq", 1)
    product_ext = jnp.concatenate([product_margin, product], 0)
    medium = causal_depthwise(product_ext.astype(jnp.float32), medium_filter, tok_rows)
    hyena_out = (filtered[:, 0] * medium).astype(jnp.bfloat16)
    head_count = chan_width // HEAD_SIZE
    score_scale = HEAD_SIZE ** (-0.5)
    seq_index = lax.axis_index("seq")
    queries = q_proj.reshape(tok_rows, head_count, HEAD_SIZE)
    query_pos = seq_index * tok_rows + jnp.arange(tok_rows, dtype=jnp.int32)
    last_query = seq_index * tok_rows + tok_rows - 1
    initial = (
        jnp.zeros((head_count, tok_rows, HEAD_SIZE), jnp.float32),
        jnp.full((head_count, tok_rows), -1e30, jnp.float32),
        jnp.zeros((head_count, tok_rows), jnp.float32),
    )
    carried = initial
    first_row = jnp.int32(0)
    key_piece = lax.all_gather(k_proj, "seq", axis=0, tiled=True)
    value_piece = lax.all_gather(hyena_out, "seq", axis=0, tiled=True)
    piece_rows = key_piece.shape[0]
    block_rows = math.gcd(piece_rows, 512)
    block_count = piece_rows // block_rows
    key_blocks = key_piece.reshape(block_count, block_rows, head_count, HEAD_SIZE)
    value_blocks = value_piece.reshape(block_count, block_rows, head_count, HEAD_SIZE)

    def visit(running, block_item):
        key_blk, value_blk, block_number = block_item
        key_start = first_row + block_number * block_rows

        def attend(current):
            weighted, run_max, total_sum = current
            scores = (
                jnp.einsum("qhd,khd->hqk", queries, key_blk, preferred_element_type=jnp.float32)
                * score_scale
            )
            key_pos = key_start + jnp.arange(block_rows, dtype=jnp.int32)
            allowed = key_pos[None, None, :] <= query_pos[None, :, None]
            masked = jnp.where(allowed, scores, -jnp.inf)
            new_max = jnp.maximum(run_max, jnp.max(masked, axis=-1))
            weights = jnp.exp(masked - new_max[..., None])
            factor = jnp.exp(run_max - new_max)
            new_total = total_sum * factor + jnp.sum(weights, axis=-1)
            new_weighted = weighted * factor[..., None] + jnp.einsum(
                "hqk,khd->hqd",
                weights.astype(jnp.bfloat16),
                value_blk,
                preferred_element_type=jnp.float32,
            )
            return (new_weighted, new_max, new_total)

        def keep_state(current):
            return current

        return (lax.cond(key_start <= last_query, attend, keep_state, running), None)

    carried, unused = lax.scan(
        visit, carried, (key_blocks, value_blocks, jnp.arange(block_count, dtype=jnp.int32))
    )
    weighted, run_max, total_sum = carried
    attended = (
        (weighted / total_sum[..., None])
        .transpose(1, 0, 2)
        .reshape(tok_rows, chan_width)
        .astype(jnp.bfloat16)
    )
    summed = lax.psum_scatter(
        lax.dot_general(
            out_weight, attended, (((0,), (1,)), ((), ())), preferred_element_type=jnp.float32
        ).astype(jnp.bfloat16),
        "head",
        scatter_dimension=0,
        tiled=True,
    ).astype(jnp.float32)
    return (hyena_out, summed.T.astype(jnp.bfloat16))


def solution(mesh):
    return jax.shard_map(
        per_device,
        mesh=mesh,
        in_specs=(
            P(("batch", "seq"), None, "head"),
            P(None, None, "head"),
            P(None, "head"),
            P(("batch", "seq"), "head"),
            P(("batch", "seq"), "head"),
            P("head", None),
        ),
        out_specs=(P(("batch", "seq"), "head"), P(("batch", "seq"), "head")),
        check_vma=False,
    )
```

profile of v0, /device:TPU:0, one launch (start us, length us, event | category | flops | bytes accessed | tf_op | source)
XLA Modules:
  0.0 636.0 jit_solution(6922452532543686896)
XLA Ops:
  7.2 0.9 slice.18
  8.1 2.4 collective-permute-start
  10.5 0.0 all-gather.5.cloned.1.call-start
  10.6 16.9 %rev.6 = f32[3,6144]{1,0:T(4,128)S(1)} reverse(f32[3,6144]{1,0:T(4,128)} %bitcast.76), dimensions={0} | reverse | bytes 147456 | tf_op jit(solution)/shard_map/rev | solution.py:19
  27.5 0.1 broadcast_in_dim.40
  27.6 7.8 %pad_maximum_fusion = bf16[514,3,2048]{2,0,1:T(8,128)(2,1)} fusion(bf16[512,3,2048]{2,0,1:T(8,128)(2,1)} %param.10, bf16[2,3,2048]{2,0,1:T(2,128)(2,1)S(1)} %collective-permute-done), kind=kLoop, calls=%fused_computation.37 | loop fusion | flops 12632064 | bytes 12632064 | tf_op jit(solution)/shard_map/concatenate | solution.py:40
  35.4 9.7 %copy.12 = bf16[514,3,2048]{0,2,1:T(8,128)(2,1)} copy(bf16[514,3,2048]{2,0,1:T(8,128)(2,1)} %pad_maximum_fusion) | data formatting | bytes 12632064 | tf_op jit(solution)/shard_map/concatenate | solution.py:40
  45.1 7.0 %pad = bf16[1,520,6144]{1,2,0:T(8,128)(2,1)} pad(bf16[1,514,6144]{1,2,0:T(8,128)(2,1)} %bitcast.69, bf16[]{:T(256)} %constant.51), padding=0_0x0_6x0_0 | pad | bytes 12705794 | tf_op jit(solution)/shard_map/broadcast_in_dim;reshape | solution.py:21
  52.1 20.5 %reshape.76 = bf16[1,8,65,6144]{2,1,3,0:T(8,128)(2,1)} reshape(bf16[1,520,6144]{1,2,0:T(8,128)(2,1)} %pad) | data formatting | bytes 12779520 | tf_op jit(solution)/shard_map/conv_general_dilated | solution.py:20
  72.7 16.8 %copy.15 = bf16[1,8,65,6144]{3,1,2,0:T(8,128)(2,1)} copy(bf16[1,8,65,6144]{2,1,3,0:T(8,128)(2,1)} %reshape.76) | data formatting | bytes 12779520 | tf_op jit(solution)/shard_map/conv_general_dilated | solution.py:20
  89.4 1.0 slice.26
  90.4 11.8 %fusion.30 = f32[8,65,6144]{2,0,1:T(8,128)} fusion(f32[3,1,6144]{2,1,0:T(1,128)S(1)} %broadcast_in_dim.40, bf16[1,7,2,6144]{3,1,2,0:T(8,128)(2,1)S(1)} %slice.26, bf16[1,8,65,6144]{3,1,2,0:T(8,128)(2,1)} %copy.15, pred[8,65]{0,1:T(8,128)(4,1)S(1)} %copy-done.4), kind=kOutput, calls=%fused_computation.33 | convolution fusion | flops 137969664 | bytes 19415560 | tf_op jit(solution)/shard_map/conv_general_dilated | solution.py:20
  102.2 17.2 %copy.16 = f32[8,65,6144]{2,1,0:T(8,128)} copy(f32[8,65,6144]{2,0,1:T(8,128)} %fusion.30) | data formatting | bytes 25559040 | tf_op jit(solution)/shard_map/conv_general_dilated | solution.py:20
  119.4 11.3 %reshape.72 = f32[1,520,6144]{2,1,0:T(8,128)} reshape(f32[8,65,6144]{2,1,0:T(8,128)} %copy.16) | data formatting | bytes 25559040 | tf_op jit(solution)/shard_map/conv_general_dilated | solution.py:20
  130.7 10.6 %slice.27 = f32[1,512,6144]{2,1,0:T(8,128)} slice(f32[1,520,6144]{2,1,0:T(8,128)} %reshape.72), slice={[0:1], [0:512], [0:6144]} | slice | bytes 25165824 | tf_op jit(solution)/shard_map/conv_general_dilated | solution.py:20
  141.3 12.8 %copy.17 = f32[1,512,6144]{1,2,0:T(8,128)} copy(f32[1,512,6144]{2,1,0:T(8,128)} %slice.27) | data formatting | bytes 25165824 | tf_op jit(solution)/shard_map/conv_general_dilated | solution.py:20
  154.0 7.7 %fusion.44 = (f32[512,1,2048]{0,2,1:T(8,128)}, bf16[512,1,2048]{0,2,1:T(8,128)(2,1)S(1)}) fusion(f32[512,3,2048]{0,2,1:T(8,128)} %bitcast.66), kind=kLoop, calls=%fused_computation.51 | loop fusion | flops 2097152 | bytes 18874368 | tf_op jit(solution)/shard_map/slice | solution.py:49
  161.8 1.0 slice_bitcast_fusion
  162.8 5.4 collective-permute-start.1
  168.2 5.2 rev.7
  173.3 5.5 copy.33
  178.8 4.0 maximum_bitcast_fusion
  182.8 11.5 %copy.20 = bf16[1,639,2048]{2,0,1:T(2,128)(2,1)} copy(bf16[1,639,2048]{1,2,0:T(8,128)(2,1)} %maximum_bitcast_fusion) | data formatting | bytes 5234688 | tf_op jit(solution)/shard_map/broadcast_in_dim | solution.py:21
  194.4 48.5 %fusion.39 = f32[1,512,2048]{2,0,1:T(1,128)S(1)} fusion(bf16[1,639,2048]{2,0,1:T(2,128)(2,1)} %copy.20, f32[128,1,2048]{2,0,1:T(8,128)S(1)} %bitcast.75), kind=kOutput, calls=%fused_computation.45 | convolution fusion | flops 1610612736 | bytes 7860224 | tf_op jit(solution)/shard_map/conv_general_dilated | solution.py:20
  242.9 2.7 fusion.37
  245.6 0.0 reduce-scatter.2.cloned.1.call-start
  245.7 2.7 copy.22
  248.4 3.0 copy.24
  251.5 10.9 %copy.34 = bf16[256,8,16,128]{3,2,1,0:T(8,128)(2,1)} copy(bf16[256,8,16,128]{3,1,2,0:T(8,128)(2,1)} %bitcast.71) | data formatting | bytes 16777216
  262.3 8.8 %copy.23 = bf16[4,512,16,128]{3,1,2,0:T(8,128)(2,1)} copy(bf16[4,512,16,128]{3,2,1,0:T(8,128)(2,1)} %bitcast.67) | data formatting | bytes 16777216
  271.2 33.2 %all-gather.5.cloned.1.call-done = bf16[2048,2048]{1,0:T(8,128)(2,1)} async-done(((bf16[512,2048]{1,0:T(8,128)(2,1)}), bf16[2048,2048]{1,0:T(8,128)(2,1)}) %all-gather.5.cloned.1.call-update) | async-done | bytes 8388624 | tf_op jit(solution)/shard_map/all_gather | solution.py:64
  304.4 9.8 %copy.35 = bf16[256,8,16,128]{3,2,1,0:T(8,128)(2,1)} copy(bf16[256,8,16,128]{3,1,2,0:T(8,128)(2,1)} %bitcast.72) | data formatting | bytes 16777216
  314.1 8.8 %copy.25 = bf16[4,512,16,128]{3,1,2,0:T(8,128)(2,1)} copy(bf16[4,512,16,128]{3,2,1,0:T(8,128)(2,1)} %bitcast.68) | data formatting | bytes 16777216
  322.9 2.5 broadcast_in_dim.43
  325.4 35.2 %while.15 = (s32[]{:T(128)}, f32[16,512,128]{2,1,0:T(8,128)}, f32[16,512]{1,0:T(8,128)S(1)}, f32[16,512]{1,0:T(8,128)S(1)}, s32[4]{0:T(128)S(1)}, /*index=5*/s32...) while((s32[]{:T(128)}, f32[16,512,128]{2,1,0:T(8,128)}, ...), condition=%wide.region_5.6_spmd.clone, body=%wide.region_0.5_spmd.clone.sunk | while | flops 2195997696 | bytes 66598184 | solution.py:101
  325.6 0.6 dynamic_slice.35
  326.9 30.0 %conditional.3 = ((f32[16,512,128]{2,1,0:T(8,128)}, f32[16,512]{1,0:T(8,128)S(1)}, f32[16,512]{1,0:T(8,128)S(1)})) conditional(s32[]{:T(128)} %convert_element_type.60, (f32[16,512,128]{2,1,0:T(8,128)}, f32[16,512]{1,0:T(8,128)S(1)}, f32[16,512]{1,0:T(8,128)S(1)}) %tuple.46, (s32[]{:T(128)}, s32[]{:T(128)}, bf16[4,512,16,128]{3,1,2,0:T(8,128)(2,1)}, ...), branch_computations={%region_1.1_spmd, %region_2.4_spmd} | conditional | flops 2195997696 | bytes 66595880 | solution.py:99
  326.9 0.2 broadcast_compare_fusion
  327.1 8.8 %fusion.4 = (f32[16,512]{1,0:T(8,128)S(1)}, f32[16,512,512]{2,1,0:T(8,128)}) fusion(pred[512,512]{0,1:T(8,128)(4,1)S(1)} %broadcast_compare_fusion, bf16[512,16,128]{2,0,1:T(8,128)(2,1)S(1)} %get-tuple-element.117, bf16[4,512,16,128]{3,1,2,0:T(8,128)(2,1)} %get-tuple-element.115, s32[]{:T(128)} %get-tuple-element.116), kind=kOutput, calls=%fused_computation.5 | convolution fusion | flops 1086316544 | bytes 21266944 | tf_op jit(solution)/shard_map/while/body/eval_jaxpr/cond/branch_1_fun/qhd,khd->hqk/dot_general | solution.py:78
  335.9 9.1 %fusion.2 = f32[16,512]{1,0:T(8,128)S(1)} fusion(f32[16,512,512]{2,1,0:T(8,128)} %get-tuple-element.212, f32[16,512]{1,0:T(8,128)S(1)} %max.4, pred[512,512]{0,1:T(8,128)(4,1)S(1)} %broadcast_compare_fusion), kind=kLoop, calls=%fused_computation.3 | loop fusion | flops 16769024 | bytes 17104896 | tf_op jit(solution)/shard_map/while/body/eval_jaxpr/cond/branch_1_fun/reduce_sum | solution.py:87
  345.1 11.7 %multiply_add_fusion = f32[16,512,128]{2,1,0:T(8,128)} fusion(f32[16,512,128]{2,1,0:T(8,128)} %get-tuple-element.111, f32[16,512]{1,0:T(8,128)S(1)} %get-tuple-element.210, bf16[4,512,16,128]{3,1,2,0:T(8,128)(2,1)} %get-tuple-element.118, s32[]{:T(128)} %get-tuple-element.116, f32[16,512,512]{2,1,0:T(8,128)} %get-tuple-element.212, f32[16,512]{1,0:T(8,128)S(1)} %max.4, ...), kind=kOutput, calls=%fused_computation.11 | convolution fusion | flops 1092616192 | bytes 27591168 | tf_op jit(solution)/shard_map/while/body/eval_jaxpr/cond/branch_1_fun/hqk,khd->hqd/dot_general | solution.py:88
  356.8 0.6 dynamic_slice.35
  358.1 0.6 dynamic_slice.35
  359.4 0.6 dynamic_slice.35
  360.6 5.4 copy.26
  366.0 2.8 divide_convert_fusion
  368.8 26.1 %fusion.25 = bf16[8192,512]{0,1:T(8,128)(2,1)} fusion(bf16[512,2048]{0,1:T(8,128)(2,1)S(1)} %bitcast.74, bf16[2048,8192]{1,0:T(8,128)(2,1)} %param.15), kind=kOutput, calls=%fused_computation.29 | convolution fusion | flops 17184063488 | bytes 44040192 | tf_op jit(solution)/shard_map/dot_general | solution.py:112
  395.0 234.0 %reduce-scatter.2.cloned.1.call-done = bf16[2048,512]{0,1:T(8,128)(2,1)} async-done(((bf16[8192,512]{0,1:T(8,128)(2,1)}), bf16[2048,512]{0,1:T(8,128)(2,1)}) %reduce-scatter.2.cloned.1.call-update) | async-done | bytes 2097168 | tf_op jit(solution)/shard_map/reduce_scatter | solution.py:111
  (31 shorter events, 0.2 us)
Async XLA Ops:
  7.2 244.3 %all-gather.3.cloned.1.call-start = ((), (), s32[]{:S(2)}) async-start(), calls=%async_computation.1 | async-start | bytes 10485760 | tf_op jit(solution)/shard_map/all_gather | solution.py:63
  8.1 19.4 %collective-permute-start = (bf16[2,3,2048]{2,0,1:T(2,128)(2,1)S(1)}, bf16[2,3,2048]{2,0,1:T(2,128)(2,1)S(1)}, u32[]{:S(2)}, u32[]{:S(2)}) collective-permute-start(bf16[2,3,2048]{2,0,1:T(2,128)(2,1)S(1)} %slice.18), channel_id=1, source_target_pairs={{0,8},{8,16},{16,24},{1,9},{9,17},{17,25},{2,10},{10,18},{18,26},{... | collective-permute-start | bytes 73736 | tf_op jit(solution)/shard_map/ppermute | solution.py:13
  10.5 293.8 %all-gather.5.cloned.1.call-start = ((), (), s32[]{:S(2)}) async-start(), calls=%async_computation.2 | async-start | bytes 10485760 | tf_op jit(solution)/shard_map/all_gather | solution.py:64
  72.7 17.8 %copy-start.4 = (pred[8,65]{0,1:T(8,128)(4,1)S(1)}, pred[8,65]{0,1:T(8,128)(4,1)}, u32[]{:S(2)}) copy-start(pred[8,65]{0,1:T(8,128)(4,1)} %constant.55) | copy-start | bytes 1564
  154.0 14.1 %copy-start.2 = (f32[128,2048]{1,0:T(8,128)S(1)}, f32[128,2048]{1,0:T(8,128)}, u32[]{:S(2)}) copy-start(f32[128,2048]{1,0:T(8,128)} %param.12) | copy-start | bytes 3145732
  162.8 16.0 %collective-permute-start.1 = (bf16[127,2048]{0,1:T(8,128)(2,1)}, bf16[127,2048]{0,1:T(8,128)(2,1)}, u32[]{:S(2)}, u32[]{:S(2)}) collective-permute-start(bf16[127,2048]{0,1:T(8,128)(2,1)} %slice_bitcast_fusion), channel_id=1, source_target_pairs={{0,8},{8,16},{16,24},{1,9},{9,17},{17,25},{2,10},{10,18},{18,26},{... | collective-permute-start | bytes 1560584 | tf_op jit(solution)/shard_map/ppermute | solution.py:13
  178.8 15.6 %copy-start.3 = (f32[128,2048]{1,0:T(8,128)S(1)}, f32[128,2048]{1,0:T(8,128)}, u32[]{:S(2)}) copy-start(f32[128,2048]{1,0:T(8,128)} %rev.7) | copy-start | bytes 3145732
  194.4 48.5 %copy-start = (f32[512,1,2048]{2,0,1:T(8,128)S(1)}, f32[512,1,2048]{2,0,1:T(8,128)}, u32[]{:S(2)}) copy-start(f32[512,1,2048]{2,0,1:T(8,128)} %copy.33) | copy-start | bytes 12582916
  242.9 2.8 copy-start.1
  245.6 383.4 %reduce-scatter.2.cloned.1.call-start = ((), (), s32[]{:S(2)}) async-start(), calls=%async_computation.3 | async-start | bytes 10485760 | tf_op jit(solution)/shard_map/reduce_scatter | solution.py:111
Sparse Core Ops, SparseCore 0:
  10.6 60.8 all-gather.2
  245.7 58.5 all-gather.4
  395.1 233.8 reduce-scatter.1
where the time goes:
time: 644 us; the launch traced here: 636 us
  waiting for transfers between devices  267 us (41%)
  local copies, waits for them, and re-layouts  202 us (31%)
  matrix products  107 us (17%)
  other arithmetic  34.5 us (5%)
  between operations  14.4 us (2%)
  starting transfers between devices  7.87 us (1%)
    reduce_scatter x1, waiting for transfers between devices, per_device(): lax.psum_scatter(lax.dot_general(out_weight, attended, (((0,), (1,)), (()...  234 us
    conv_general_dilated x7, local copies, waits for them, and re-layouts, causal_depthwise(): lax.conv_general_dilated(window[None], kernel, (1,), 'VALID', feature_gro...  90.1 us
    conv_general_dilated x2, matrix products, causal_depthwise(): lax.conv_general_dilated(window[None], kernel, (1,), 'VALID', feature_gro...  60.3 us
    unnamed x17, local copies, waits for them, and re-layouts  49.5 us
    all_gather x1, waiting for transfers between devices, per_device(): value_piece = lax.all_gather(hyena_out, 'seq', axis=0, tiled=True)  33.2 us
    dot_general x1, matrix products, per_device(): lax.dot_general(out_weight, attended, (((0,), (1,)), ((), ())), preferred...  26.1 us
    rev x2, local copies, waits for them, and re-layouts, causal_depthwise(): kernel = taps[::-1][:, None, :]  22.1 us
  transfers between devices with their start and end apart: 5, of which 2 were waited for; matrix products, arithmetic and copies ran while one was open for 40% of the time, Pallas kernels for 0%

commit v1 on v0

--- a/solution.py
+++ b/solution.py
@@ -61,7 +61,17 @@
     carried = initial
     first_row = jnp.int32(0)
     key_piece = lax.all_gather(k_proj, "seq", axis=0, tiled=True)
-    value_piece = lax.all_gather(hyena_out, "seq", axis=0, tiled=True)
+    o_now = lax.axis_size("seq")
+    g_now = lax.axis_index("seq")
+    val2, tmp = (o_now, g_now)
+    value_piece, reached = (hyena_out, 1)
+    while reached < val2:
+        field_out = tuple(((j, j ^ reached) for j in range(val2)))
+        passed = lax.ppermute(value_piece, "seq", field_out)
+        b_now = jnp.concatenate([value_piece, passed], 0)
+        moved = jnp.concatenate([passed, value_piece], 0)
+        value_piece = jnp.where(tmp & reached == 0, b_now, moved)
+        reached = 2 * reached
     piece_rows = key_piece.shape[0]
     block_rows = math.gcd(piece_rows, 512)
     block_count = piece_rows // block_rows

time: 644 us -> 715 us (1.11)
  waiting for transfers between devices: 267 us -> 324 us
  other arithmetic: 34.5 us -> 49.8 us
    ppermute x0 -> x2, waiting for transfers between devices: none -> 90.2 us  [per_device(): passed = lax.ppermute(value_piece, 'seq', field_out)]
    all_gather x1 -> x0, waiting for transfers between devices: 33.2 us -> none  [per_device(): value_piece = lax.all_gather(hyena_out, 'seq', axis=0, tiled=True)]
    unnamed x0 -> x1, other arithmetic: none -> 10.2 us
  transfers between devices with their start and end apart: 5 -> 6, of which waited for: 2 -> 3; matrix products, arithmetic and copies ran while one was open for 40% -> 19% of each run, Pallas kernels for 0% -> 0%
where the time goes in v1:
time: 715 us; the launch traced here: 707 us
  waiting for transfers between devices  324 us (45%)
  local copies, waits for them, and re-layouts  202 us (28%)
  matrix products  106 us (15%)
  other arithmetic  49.8 us (7%)
  between operations  14.4 us (2%)
  starting transfers between devices  7.83 us (1%)
    reduce_scatter x1, waiting for transfers between devices, per_device(): lax.psum_scatter(lax.dot_general(out_weight, attended, (((0,), (1,)), (()...  233 us
    ppermute x2, waiting for transfers between devices, per_device(): passed = lax.ppermute(value_piece, 'seq', field_out)  90.2 us
    conv_general_dilated x7, local copies, waits for them, and re-layouts, causal_depthwise(): lax.conv_general_dilated(window[None], kernel, (1,), 'VALID', feature_gro...  90.1 us
    conv_general_dilated x2, matrix products, causal_depthwise(): lax.conv_general_dilated(window[None], kernel, (1,), 'VALID', feature_gro...  60 us
    unnamed x17, local copies, waits for them, and re-layouts  49.8 us
    dot_general x1, matrix products, per_device(): lax.dot_general(out_weight, attended, (((0,), (1,)), ((), ())), preferred...  26 us
    rev x2, local copies, waits for them, and re-layouts, causal_depthwise(): kernel = taps[::-1][:, None, :]  22 us
  transfers between devices with their start and end apart: 6, of which 3 were waited for; matrix products, arithmetic and copies ran while one was open for 19% of the time, Pallas kernels for 0%

profile of v1, /device:TPU:0, one launch (start us, length us, event | category | flops | bytes accessed | tf_op | source)
XLA Modules:
  0.0 707.3 jit_solution(401534202147556825)
XLA Ops:
  7.2 0.9 slice.18
  8.1 2.4 collective-permute-start
  10.5 16.9 %rev.6 = f32[3,6144]{1,0:T(4,128)S(1)} reverse(f32[3,6144]{1,0:T(4,128)} %bitcast.76), dimensions={0} | reverse | bytes 147456 | tf_op jit(solution)/shard_map/rev | solution.py:19
  27.4 7.9 %pad_maximum_fusion = bf16[514,3,2048]{2,0,1:T(8,128)(2,1)} fusion(bf16[512,3,2048]{2,0,1:T(8,128)(2,1)} %param.10, bf16[2,3,2048]{2,0,1:T(2,128)(2,1)S(1)} %collective-permute-done), kind=kLoop, calls=%fused_computation.39 | loop fusion | flops 12632064 | bytes 12632064 | tf_op jit(solution)/shard_map/concatenate | solution.py:40
  35.3 9.7 %copy.12 = bf16[514,3,2048]{0,2,1:T(8,128)(2,1)} copy(bf16[514,3,2048]{2,0,1:T(8,128)(2,1)} %pad_maximum_fusion) | data formatting | bytes 12632064 | tf_op jit(solution)/shard_map/concatenate | solution.py:40
  45.0 7.0 pad
  52.0 20.5 %reshape.77 = bf16[1,8,65,6144]{2,1,3,0:T(8,128)(2,1)} reshape(bf16[1,520,6144]{1,2,0:T(8,128)(2,1)} %pad) | data formatting | bytes 12779520 | tf_op jit(solution)/shard_map/conv_general_dilated | solution.py:20
  72.5 16.8 %copy.15 = bf16[1,8,65,6144]{3,1,2,0:T(8,128)(2,1)} copy(bf16[1,8,65,6144]{2,1,3,0:T(8,128)(2,1)} %reshape.77) | data formatting | bytes 12779520 | tf_op jit(solution)/shard_map/conv_general_dilated | solution.py:20
  89.3 1.0 slice.26
  90.3 11.5 %fusion.31 = f32[8,65,6144]{2,0,1:T(8,128)} fusion(f32[3,1,6144]{2,1,0:T(1,128)S(1)} %broadcast_in_dim.40, bf16[1,7,2,6144]{3,1,2,0:T(8,128)(2,1)S(1)} %slice.26, bf16[1,8,65,6144]{3,1,2,0:T(8,128)(2,1)} %copy.15, pred[8,65]{0,1:T(8,128)(4,1)S(1)} %copy-done.4), kind=kOutput, calls=%fused_computation.35 | convolution fusion | flops 137969664 | bytes 19415560 | tf_op jit(solution)/shard_map/conv_general_dilated | solution.py:20
  101.9 17.2 %copy.16 = f32[8,65,6144]{2,1,0:T(8,128)} copy(f32[8,65,6144]{2,0,1:T(8,128)} %fusion.31) | data formatting | bytes 25559040 | tf_op jit(solution)/shard_map/conv_general_dilated | solution.py:20
  119.1 11.2 %reshape.73 = f32[1,520,6144]{2,1,0:T(8,128)} reshape(f32[8,65,6144]{2,1,0:T(8,128)} %copy.16) | data formatting | bytes 25559040 | tf_op jit(solution)/shard_map/conv_general_dilated | solution.py:20
  130.3 10.6 %slice.27 = f32[1,512,6144]{2,1,0:T(8,128)} slice(f32[1,520,6144]{2,1,0:T(8,128)} %reshape.73), slice={[0:1], [0:512], [0:6144]} | slice | bytes 25165824 | tf_op jit(solution)/shard_map/conv_general_dilated | solution.py:20
  140.9 12.8 %copy.17 = f32[1,512,6144]{1,2,0:T(8,128)} copy(f32[1,512,6144]{2,1,0:T(8,128)} %slice.27) | data formatting | bytes 25165824 | tf_op jit(solution)/shard_map/conv_general_dilated | solution.py:20
  153.7 7.7 %fusion.45 = (f32[512,1,2048]{0,2,1:T(8,128)}, bf16[512,1,2048]{0,2,1:T(8,128)(2,1)S(1)}) fusion(f32[512,3,2048]{0,2,1:T(8,128)} %bitcast.67), kind=kLoop, calls=%fused_computation.54 | loop fusion | flops 2097152 | bytes 18874368 | tf_op jit(solution)/shard_map/slice | solution.py:49
  161.4 1.0 slice_bitcast_fusion
  162.4 5.3 collective-permute-start.1
  167.8 5.2 rev.7
  173.0 5.8 copy.33
  178.8 4.2 maximum_bitcast_fusion
  183.1 11.5 %copy.20 = bf16[1,639,2048]{2,0,1:T(2,128)(2,1)} copy(bf16[1,639,2048]{1,2,0:T(8,128)(2,1)} %maximum_bitcast_fusion) | data formatting | bytes 5234688 | tf_op jit(solution)/shard_map/broadcast_in_dim | solution.py:21
  194.6 48.5 %fusion.40 = f32[1,512,2048]{2,0,1:T(1,128)S(1)} fusion(bf16[1,639,2048]{2,0,1:T(2,128)(2,1)} %copy.20, f32[128,1,2048]{2,0,1:T(8,128)S(1)} %bitcast.75), kind=kOutput, calls=%fused_computation.48 | convolution fusion | flops 1610612736 | bytes 7860224 | tf_op jit(solution)/shard_map/conv_general_dilated | solution.py:20
  243.1 2.4 fusion.38
  245.6 4.3 collective-permute-done.2
  249.8 5.2 maximum_select_fusion.1
  255.1 3.9 copy.22
  259.0 3.0 copy.24
  262.1 86.0 %collective-permute-done.3 = bf16[1024,2048]{1,0:T(8,128)(2,1)} collective-permute-done((bf16[1024,2048]{1,0:T(8,128)(2,1)}, bf16[1024,2048]{1,0:T(8,128)(2,1)}, u32[]{:S(2)}, u32[]{:S(2)}) %collective-permute-start.3) | collective-permute-done | bytes 4194336 | tf_op jit(solution)/shard_map/ppermute | solution.py:70
  348.0 10.2 %fusion.26 = bf16[256,8,16,128]{3,1,2,0:T(8,128)(2,1)} fusion(bf16[1024,2048]{1,0:T(8,128)(2,1)} %collective-permute-done.3, bf16[1024,2048]{1,0:T(8,128)(2,1)} %maximum_select_fusion.1, pred[]{:T(512)S(6)} %eq.6), kind=kLoop, calls=%fused_computation.31 | loop fusion | flops 37748736 | bytes 16777216
  358.3 9.8 %copy.35 = bf16[256,8,16,128]{3,2,1,0:T(8,128)(2,1)} copy(bf16[256,8,16,128]{3,1,2,0:T(8,128)(2,1)} %fusion.26) | data formatting | bytes 16777216
  368.0 8.8 %copy.25 = bf16[4,512,16,128]{3,1,2,0:T(8,128)(2,1)} copy(bf16[4,512,16,128]{3,2,1,0:T(8,128)(2,1)} %bitcast.68) | data formatting | bytes 16777216
  376.8 9.8 %copy.34 = bf16[256,8,16,128]{3,2,1,0:T(8,128)(2,1)} copy(bf16[256,8,16,128]{3,1,2,0:T(8,128)(2,1)} %bitcast.72) | data formatting | bytes 16777216
  386.6 8.8 %copy.23 = bf16[4,512,16,128]{3,1,2,0:T(8,128)(2,1)} copy(bf16[4,512,16,128]{3,2,1,0:T(8,128)(2,1)} %bitcast.69) | data formatting | bytes 16777216
  395.3 2.5 broadcast_in_dim.43
  397.8 34.7 %while.15 = (s32[]{:T(128)}, f32[16,512,128]{2,1,0:T(8,128)}, f32[16,512]{1,0:T(8,128)S(1)}, f32[16,512]{1,0:T(8,128)S(1)}, s32[4]{0:T(128)S(1)}, /*index=5*/s32...) while((s32[]{:T(128)}, f32[16,512,128]{2,1,0:T(8,128)}, ...), condition=%wide.region_5.6_spmd.clone, body=%wide.region_0.5_spmd.clone.sunk | while | flops 2195997696 | bytes 66598184 | solution.py:111
  398.0 0.6 dynamic_slice.35
  399.2 29.9 %conditional.3 = ((f32[16,512,128]{2,1,0:T(8,128)}, f32[16,512]{1,0:T(8,128)S(1)}, f32[16,512]{1,0:T(8,128)S(1)})) conditional(s32[]{:T(128)} %convert_element_type.60, (f32[16,512,128]{2,1,0:T(8,128)}, f32[16,512]{1,0:T(8,128)S(1)}, f32[16,512]{1,0:T(8,128)S(1)}) %tuple.46, (s32[]{:T(128)}, s32[]{:T(128)}, bf16[4,512,16,128]{3,1,2,0:T(8,128)(2,1)}, ...), branch_computations={%region_1.1_spmd, %region_2.4_spmd} | conditional | flops 2195997696 | bytes 66595880 | solution.py:109
  399.2 0.2 broadcast_compare_fusion
  399.4 8.8 %fusion.4 = (f32[16,512]{1,0:T(8,128)S(1)}, f32[16,512,512]{2,1,0:T(8,128)}) fusion(pred[512,512]{0,1:T(8,128)(4,1)S(1)} %broadcast_compare_fusion, bf16[512,16,128]{2,0,1:T(8,128)(2,1)S(1)} %get-tuple-element.117, bf16[4,512,16,128]{3,1,2,0:T(8,128)(2,1)} %get-tuple-element.115, s32[]{:T(128)} %get-tuple-element.116), kind=kOutput, calls=%fused_computation.5 | convolution fusion | flops 1086316544 | bytes 21266944 | tf_op jit(solution)/shard_map/while/body/eval_jaxpr/cond/branch_1_fun/qhd,khd->hqk/dot_general | solution.py:88
  408.2 9.1 %fusion.2 = f32[16,512]{1,0:T(8,128)S(1)} fusion(f32[16,512,512]{2,1,0:T(8,128)} %get-tuple-element.212, f32[16,512]{1,0:T(8,128)S(1)} %max.4, pred[512,512]{0,1:T(8,128)(4,1)S(1)} %broadcast_compare_fusion), kind=kLoop, calls=%fused_computation.3 | loop fusion | flops 16769024 | bytes 17104896 | tf_op jit(solution)/shard_map/while/body/eval_jaxpr/cond/branch_1_fun/reduce_sum | solution.py:97
  417.4 11.7 %multiply_add_fusion = f32[16,512,128]{2,1,0:T(8,128)} fusion(f32[16,512,128]{2,1,0:T(8,128)} %get-tuple-element.111, f32[16,512]{1,0:T(8,128)S(1)} %get-tuple-element.210, bf16[4,512,16,128]{3,1,2,0:T(8,128)(2,1)} %get-tuple-element.118, s32[]{:T(128)} %get-tuple-element.116, f32[16,512,512]{2,1,0:T(8,128)} %get-tuple-element.212, f32[16,512]{1,0:T(8,128)S(1)} %max.4, ...), kind=kOutput, calls=%fused_computation.11 | convolution fusion | flops 1092616192 | bytes 27591168 | tf_op jit(solution)/shard_map/while/body/eval_jaxpr/cond/branch_1_fun/hqk,khd->hqd/dot_general | solution.py:98
  429.0 0.6 dynamic_slice.35
  430.2 0.6 dynamic_slice.35
  431.4 0.6 dynamic_slice.35
  432.6 5.4 copy.26
  437.9 2.8 divide_convert_fusion
  440.7 26.0 %fusion.25 = bf16[8192,512]{0,1:T(8,128)(2,1)} fusion(bf16[512,2048]{0,1:T(8,128)(2,1)S(1)} %bitcast.74, bf16[2048,8192]{1,0:T(8,128)(2,1)} %param.15), kind=kOutput, calls=%fused_computation.29 | convolution fusion | flops 17184063488 | bytes 44040192 | tf_op jit(solution)/shard_map/dot_general | solution.py:122
  466.8 233.4 %reduce-scatter.2.cloned.1.call-done = bf16[2048,512]{0,1:T(8,128)(2,1)} async-done(((bf16[8192,512]{0,1:T(8,128)(2,1)}), bf16[2048,512]{0,1:T(8,128)(2,1)}) %reduce-scatter.2.cloned.1.call-update) | async-done | bytes 2097168 | tf_op jit(solution)/shard_map/reduce_scatter | solution.py:121
  (34 shorter events, 0.4 us)
Async XLA Ops:
  7.2 369.6 %all-gather.2.cloned.1.call-start = ((), (), s32[]{:S(2)}) async-start(), calls=%async_computation.1 | async-start | bytes 10485760 | tf_op jit(solution)/shard_map/all_gather | solution.py:63
  8.1 19.3 %collective-permute-start = (bf16[2,3,2048]{2,0,1:T(2,128)(2,1)S(1)}, bf16[2,3,2048]{2,0,1:T(2,128)(2,1)S(1)}, u32[]{:S(2)}, u32[]{:S(2)}) collective-permute-start(bf16[2,3,2048]{2,0,1:T(2,128)(2,1)S(1)} %slice.18), channel_id=1, source_target_pairs={{0,8},{8,16},{16,24},{1,9},{9,17},{17,25},{2,10},{10,18},{18,26},{... | collective-permute-start | bytes 73736 | tf_op jit(solution)/shard_map/ppermute | solution.py:13
  72.5 17.8 %copy-start.4 = (pred[8,65]{0,1:T(8,128)(4,1)S(1)}, pred[8,65]{0,1:T(8,128)(4,1)}, u32[]{:S(2)}) copy-start(pred[8,65]{0,1:T(8,128)(4,1)} %constant.58) | copy-start | bytes 1564
  153.7 14.1 %copy-start.2 = (f32[128,2048]{1,0:T(8,128)S(1)}, f32[128,2048]{1,0:T(8,128)}, u32[]{:S(2)}) copy-start(f32[128,2048]{1,0:T(8,128)} %param.12) | copy-start | bytes 3145732
  162.4 16.4 %collective-permute-start.1 = (bf16[127,2048]{0,1:T(8,128)(2,1)}, bf16[127,2048]{0,1:T(8,128)(2,1)}, u32[]{:S(2)}, u32[]{:S(2)}) collective-permute-start(bf16[127,2048]{0,1:T(8,128)(2,1)} %slice_bitcast_fusion), channel_id=1, source_target_pairs={{0,8},{8,16},{16,24},{1,9},{9,17},{17,25},{2,10},{10,18},{18,26},{... | collective-permute-start | bytes 1560584 | tf_op jit(solution)/shard_map/ppermute | solution.py:13
  167.8 532.4 %reduce-scatter.2.cloned.1.call-start = ((), (), s32[]{:S(2)}) async-start(), calls=%async_computation.2 | async-start | bytes 10485760 | tf_op jit(solution)/shard_map/reduce_scatter | solution.py:121
  178.8 15.8 %copy-start.3 = (f32[128,2048]{1,0:T(8,128)S(1)}, f32[128,2048]{1,0:T(8,128)}, u32[]{:S(2)}) copy-start(f32[128,2048]{1,0:T(8,128)} %rev.7) | copy-start | bytes 3145732
  194.6 48.5 %copy-start = (f32[512,1,2048]{2,0,1:T(8,128)S(1)}, f32[512,1,2048]{2,0,1:T(8,128)}, u32[]{:S(2)}) copy-start(f32[512,1,2048]{2,0,1:T(8,128)} %copy.33) | copy-start | bytes 12582916
  245.5 13.5 %copy-start.1 = (bf16[512,2048]{1,0:T(8,128)(2,1)}, bf16[512,2048]{1,0:T(8,128)(2,1)S(1)}, u32[]{:S(2)}) copy-start(bf16[512,2048]{1,0:T(8,128)(2,1)S(1)} %fusion.38) | copy-start | bytes 6291460
  245.5 4.4 collective-permute-start.2
  255.1 92.9 %collective-permute-start.3 = (bf16[1024,2048]{1,0:T(8,128)(2,1)}, bf16[1024,2048]{1,0:T(8,128)(2,1)}, u32[]{:S(2)}, u32[]{:S(2)}) collective-permute-start(bf16[1024,2048]{1,0:T(8,128)(2,1)} %maximum_select_fusion.1), channel_id=1, source_target_pairs={{0,16},{8,24},{16,0},{24,8},{1,17},{9,25},{17,1},{25,9},{2,18},{10... | collective-permute-start | bytes 12582920 | tf_op jit(solution)/shard_map/ppermute | solution.py:70
Sparse Core Ops, SparseCore 0:
  167.9 58.5 all-gather.1
  466.9 233.2 reduce-scatter.1
